TPU v7x, 128 devices: a whole 4x4x4 slice. The times are simulated.
128 devices in a mesh: dev: 128 (over z, x, y, core).
Axes of the slice: x: 4, y: 4, z: 4, core: 2. Of those that a mesh axis runs over, the one named last changes fastest.
Arguments:
- features: float32 [65536, 256], P('dev'), may hold values from -6 to 6
- keep: int32 [65536], P('dev'), may hold values 0 or 1
- theta_one: float32 [256, 256], replicated, may hold values from -0.375 to 0.375
- theta_two: float32 [256, 256], replicated, may hold values from -0.375 to 0.375
- cotangent: float32 [65536, 256], P('dev'), may hold values from -6 to 6
- send_node: int32 [128, 128, 4], P('dev'), may hold values from 0 to 511
- recv_edge: int32 [128, 128, 4], P('dev'), may hold values from 0 to 255
- send_count: int32 [128, 128], P('dev'), may hold values from 0 to 4, as said below
Outputs:
- grad_features: float32 [65536, 256], P('dev')
- grad_theta_one: float32 [256, 256], replicated
- grad_theta_two: float32 [256, 256], replicated
Inputs may be any that keep to these rules, and one draw needn't show every extreme that they name: `send_count`: each source device has 4 live slots to at least one destination.
All inputs are finite; a program needn't handle non-finite values. No bound on the sum of `keep` on one device may be relied on, other than what follows from the above.
Results may differ from a plain program's by a relative error of at most 0.0003.
Values sent between devices are 32-bit elements; how exact they have to be, the bound alone decides.
A program may use at most 64 MiB of HBM per device.

v0:
```python
import functools

import jax
import jax.numpy as jnp
from jax import lax
from jax.experimental import pallas as pl
from jax.experimental.pallas import tpu as pltpu
from jax.sharding import PartitionSpec as P

MESH = pl.DeviceIdType.MESH
F32, BF16 = jnp.float32, jnp.bfloat16
UNROLL = 8
A_DOWN, B_DOWN, A_UP, B_UP, C_DOWN, C_UP, PAIR_IN, SCATTER, GATHER, PAIR_OUT = range(10)


def split(x):
    high = x.astype(BF16)
    return high, (x - high.astype(F32)).astype(BF16)


def dot(left, right, dims=((1,), (0,))):
    return lax.dot_general(left, right, (dims, ((), ())), preferred_element_type=F32)


def pick(onehot, x):
    high, low = split(x)
    return dot(onehot, high) + dot(onehot, low)


def matmul(left, right, dims=((1,), (0,))):
    lh, ll = split(left)
    rh, rl = split(right)
    return dot(lh, rh, dims) + (dot(lh, rl, dims) + dot(ll, rh, dims))


def kernel(
    n, slots, features, keep, theta_one, theta_two, cotangent, send_node, recv_edge, send_count,
    grad_features, grad_one, grad_two,
    gather, spread, meet, out, back, terms, partner, pair_sum, parts, total, send_sem, recv_sem,
):
    me = lax.axis_index("dev")
    core, chip, chips = lax.rem(me, 2), me // 2, n // 2
    other = me + 1 - 2 * core
    nodes, width = features.shape
    lanes = width // 2
    tile = 2 * slots

    barrier = pltpu.get_barrier_semaphore()

    def greet(_, peer):
        peer = lax.rem(peer + 1, n)
        pl.semaphore_signal(barrier, inc=1, device_id=(peer,), device_id_type=MESH)
        return peer

    lax.fori_loop(0, n - 1, greet, me, unroll=UNROLL)

    def block(index, rows=tile):
        return pl.ds(pl.multiple_of(index * rows, rows), rows)

    def exchange(phase, src, dst):
        def push(_, peer):
            peer = lax.rem(peer + 1, n)
            pltpu.make_async_remote_copy(
                src_ref=src.at[block(peer)],
                dst_ref=dst.at[block(me)],
                send_sem=send_sem.at[phase],
                recv_sem=recv_sem.at[phase],
                device_id=(peer,),
                device_id_type=MESH,
            ).start()
            return peer

        lax.fori_loop(0, n - 1, push, me, unroll=UNROLL)
        pltpu.make_async_copy(src.at[block(me)], dst.at[block(me)], recv_sem.at[phase]).start()

    def chip_exchange(phase, src_block, dst):
        def push(_, peer):
            peer = lax.rem(peer + 2, n)
            pltpu.make_async_remote_copy(
                src_ref=src_block(peer // 2),
                dst_ref=dst.at[block(chip)],
                send_sem=send_sem.at[phase],
                recv_sem=recv_sem.at[phase],
                device_id=(peer,),
                device_id_type=MESH,
            ).start()
            return peer

        lax.fori_loop(0, chips - 1, push, me, unroll=UNROLL)
        pltpu.make_async_copy(src_block(chip), dst.at[block(chip)], recv_sem.at[phase]).start()

    def arrived(phase, ref):
        pltpu.make_async_copy(ref, ref, recv_sem.at[phase]).wait()

    def sent(phase, ref):
        pltpu.make_async_copy(ref, ref, send_sem.at[phase]).wait()

    def put(ref, j, rows):
        for h in range(2):
            ref[pl.ds(h * slots + j, n, stride=tile), :] = rows[:, h * lanes : (h + 1) * lanes]

    def get(ref, j):
        return [ref[pl.ds(h * slots + j, n, stride=tile), :] for h in range(2)]

    def take(ref):
        return jnp.concatenate([jnp.concatenate(get(ref, j), axis=1) for j in range(slots)], axis=0)

    eye = lax.broadcasted_iota(jnp.int32, (n, n), 0) == lax.broadcasted_iota(jnp.int32, (n, n), 1)

    def as_row(column):
        return jnp.sum(jnp.where(eye, column, 0.0), axis=0, keepdims=True)

    def as_column(row):
        return jnp.sum(jnp.where(eye, row, 0.0), axis=1, keepdims=True)

    count = send_count[...].astype(F32)
    node_of = send_node[0].astype(F32)
    edge_of = recv_edge[0].astype(F32)
    node_lane = lax.broadcasted_iota(jnp.int32, (n, nodes), 1).astype(F32)
    node_row = lax.broadcasted_iota(jnp.int32, (nodes, n), 0).astype(F32)
    degree = jnp.zeros((nodes, n), F32)
    live = []
    for j in range(slots):
        mine = jnp.where(count > j, node_of[j : j + 1], -1.0)
        mine_column = as_column(mine)
        live.append(mine_column >= 0.0)
        gather[j * n : (j + 1) * n, :] = (node_lane == mine_column).astype(F32).astype(BF16)
        here = (node_row == mine).astype(F32)
        degree += here
        spread[:, j * n : (j + 1) * n] = here.astype(BF16)
    edge_cols = [as_column(edge_of[j : j + 1]) for j in range(slots)]
    edge_row = jnp.concatenate([edge_of[j : j + 1] for j in range(slots)], axis=1)
    for j in range(slots):
        meet[j * n : (j + 1) * n, :] = (edge_row == edge_cols[j]).astype(F32).astype(BF16)
    degree = jnp.sum(degree, axis=1, keepdims=True)
    node_scale = 1.0 / jnp.sqrt(jnp.maximum(degree, 1.0))
    keep_rows = keep[...].astype(F32)
    keep_f = jnp.concatenate([as_column(keep_rows[r : r + 1]) for r in range(nodes // n)], axis=0)

    def load_out(ref, field, mark):
        rows = pick(gather[...], field * node_scale)
        for j in range(slots):
            part = rows[j * n : (j + 1) * n]
            put(ref, j, jnp.where(live[j], part, jnp.inf) if mark else part)

    load_out(out.at[A_DOWN], features[...] * keep_f, True)
    pl.semaphore_wait(barrier, n - 1)
    exchange(A_DOWN, out.at[A_DOWN], back.at[A_DOWN])
    load_out(out.at[B_DOWN], cotangent[...], False)
    exchange(B_DOWN, out.at[B_DOWN], back.at[B_DOWN])

    arrived(A_DOWN, back.at[A_DOWN])
    fields, alive = [], []
    for j in range(slots):
        halves = get(back.at[A_DOWN], j)
        is_live = halves[0][:, :1] < jnp.inf
        alive.append(is_live.astype(F32))
        fields.append(jnp.where(is_live, jnp.concatenate(halves, axis=1), 0.0))
    alive_row = jnp.concatenate([as_row(a) for a in alive], axis=1)
    edge_scale = []
    for j in range(slots):
        shared = jnp.where(edge_row == edge_cols[j], alive_row, 0.0)
        edge_scale.append(1.0 / jnp.maximum(jnp.sum(shared, axis=1, keepdims=True), 1.0))

    def load_back(ref, field):
        rows = pick(meet[...], field)
        for j in range(slots):
            put(ref, j, rows[j * n : (j + 1) * n] * edge_scale[j])

    load_back(out.at[A_UP], jnp.concatenate(fields, axis=0))
    exchange(A_UP, out.at[A_UP], back.at[A_UP])
    arrived(B_DOWN, back.at[B_DOWN])
    load_back(out.at[B_UP], take(back.at[B_DOWN]))
    exchange(B_UP, out.at[B_UP], back.at[B_UP])

    arrived(A_UP, back.at[A_UP])
    spread_in = pick(spread[...], take(back.at[A_UP])) * node_scale
    pre = matmul(spread_in, theta_one[...])
    grow = jnp.exp(jnp.minimum(pre, 0.0))
    hidden = jnp.where(pre > 0, pre, grow - 1.0)
    slope = jnp.where(pre > 0, 1.0, grow)
    arrived(B_UP, back.at[B_UP])
    spread_cot = pick(spread[...], take(back.at[B_UP])) * node_scale
    grad_pre = matmul(spread_cot, theta_two[...], ((1,), (1,))) * slope
    load_out(out.at[C_DOWN], grad_pre, False)
    exchange(C_DOWN, out.at[C_DOWN], back.at[C_DOWN])

    term_one = matmul(spread_in, grad_pre, ((0,), (0,)))
    term_two = matmul(hidden, spread_cot, ((0,), (0,)))
    for k, term in enumerate((term_one, term_two)):
        for h in range(2):
            terms[k, h * width : (h + 1) * width, :] = term[:, h * lanes : (h + 1) * lanes]
    pltpu.make_async_remote_copy(
        src_ref=terms.at[1 - core],
        dst_ref=partner,
        send_sem=send_sem.at[PAIR_IN],
        recv_sem=recv_sem.at[PAIR_IN],
        device_id=(other,),
        device_id_type=MESH,
    ).start()
    arrived(PAIR_IN, partner)
    pair_sum[...] = terms[core] + partner[...]
    chip_exchange(SCATTER, lambda q: pair_sum.at[block(q)], parts)

    arrived(C_DOWN, back.at[C_DOWN])
    load_back(out.at[C_UP], take(back.at[C_DOWN]))
    exchange(C_UP, out.at[C_UP], back.at[C_UP])

    arrived(SCATTER, parts)
    sent(SCATTER, parts.at[pl.ds(0, (chips - 1) * tile)])
    norm_factor = 1.0 / jnp.sqrt(jnp.float32(nodes * n))
    summed = jnp.sum(parts[...].reshape(chips, tile, lanes), axis=0) * norm_factor
    pair_sum[:tile, :] = summed
    chip_exchange(GATHER, lambda q: pair_sum.at[pl.ds(0, tile)], total.at[core])

    arrived(C_UP, back.at[C_UP])
    spread_grad = pick(spread[...], take(back.at[C_UP])) * node_scale
    grad_features[...] = matmul(spread_grad, theta_one[...], ((1,), (1,))) * keep_f

    arrived(GATHER, total.at[core])
    pltpu.make_async_remote_copy(
        src_ref=total.at[core],
        dst_ref=total.at[core],
        send_sem=send_sem.at[PAIR_OUT],
        recv_sem=recv_sem.at[PAIR_OUT],
        device_id=(other,),
        device_id_type=MESH,
    ).start()
    for phase in (A_DOWN, B_DOWN, A_UP, B_UP, C_DOWN, C_UP):
        sent(phase, out.at[phase, pl.ds(0, (n - 1) * tile)])
    sent(PAIR_IN, partner)
    sent(GATHER, parts.at[pl.ds(0, (chips - 1) * tile)])
    sent(PAIR_OUT, partner)
    arrived(PAIR_OUT, partner)
    for k, ref in enumerate((grad_one, grad_two)):
        for h in range(2):
            ref[:, h * lanes : (h + 1) * lanes] = total[k, h * width : (h + 1) * width, :]


def solution(mesh):
    n = mesh.shape["dev"]

    def body(features, keep, theta_one, theta_two, cotangent, send_node, recv_edge, send_count):
        nodes, width = features.shape
        slots = send_node.shape[2]
        rows = n * 2 * slots
        whole = pl.BlockSpec(memory_space=pltpu.VMEM)
        return pl.pallas_call(
            functools.partial(kernel, n, slots),
            out_shape=(
                jax.ShapeDtypeStruct((nodes, width), F32),
                jax.ShapeDtypeStruct((width, width), F32),
                jax.ShapeDtypeStruct((width, width), F32),
            ),
            in_specs=[whole] * 8,
            out_specs=(whole,) * 3,
            scratch_shapes=[
                pltpu.VMEM((slots * n, nodes), BF16),
                pltpu.VMEM((nodes, slots * n), BF16),
                pltpu.VMEM((slots * n, slots * n), BF16),
                pltpu.VMEM((6, rows, width // 2), F32),
                pltpu.VMEM((6, rows, width // 2), F32),
                pltpu.VMEM((2, 2 * width, width // 2), F32),
                pltpu.VMEM((2 * width, width // 2), F32),
                pltpu.VMEM((2 * width, width // 2), F32),
                pltpu.VMEM((2 * width, width // 2), F32),
                pltpu.VMEM((2, 2 * width, width // 2), F32),
                pltpu.SemaphoreType.DMA((10,)),
                pltpu.SemaphoreType.DMA((10,)),
            ],
            compiler_params=pltpu.CompilerParams(
                collective_id=0, has_side_effects=True, vmem_limit_bytes=48 << 20
            ),
        )(
            features, keep.reshape(nodes // n, n), theta_one, theta_two, cotangent,
            send_node.transpose(0, 2, 1), recv_edge.transpose(0, 2, 1), send_count,
        )

    placed = (
        P("dev", None),
        P("dev"),
        P(),
        P(),
        P("dev", None),
        P("dev", None, None),
        P("dev", None, None),
        P("dev", None),
    )
    return jax.shard_map(
        body, mesh=mesh, in_specs=placed, out_specs=(P("dev", None), P(), P()), check_vma=False
    )
```

profile of v0, /device:TPU:1, one launch (start us, length us, event | category | flops | bytes accessed | tf_op | source)
XLA Modules:
  0.0 76.8 jit_solution(10835849095705353625)
XLA Ops:
  0.6 0.0 copy-start.5
  0.6 0.0 copy-start.4
  0.7 0.0 copy-start.7
  0.7 0.7 copy-done.5
  1.3 0.0 copy-done.4
  1.3 0.0 copy-done.7
  1.3 0.0 copy-start
  1.3 1.0 %copy-done = f32[512,256]{1,0:T(8,128)S(1)} copy-done((f32[512,256]{1,0:T(8,128)S(1)}, f32[512,256]{1,0:T(8,128)}, u32[]{:S(2)}) %copy-start) | copy-done | bytes 524312
  2.4 0.0 copy-start.1
  2.4 1.0 %copy-done.1 = f32[512,256]{1,0:T(8,128)S(1)} copy-done((f32[512,256]{1,0:T(8,128)S(1)}, f32[512,256]{1,0:T(8,128)}, u32[]{:S(2)}) %copy-start.1) | copy-done | bytes 524312
  3.4 0.0 copy-start.2
  3.4 0.9 %copy-done.2 = f32[256,256]{1,0:T(8,128)S(1)} copy-done((f32[256,256]{1,0:T(8,128)S(1)}, f32[256,256]{1,0:T(8,128)}, u32[]{:S(2)}) %copy-start.2) | copy-done | bytes 262168
  4.4 0.0 copy-start.3
  4.4 0.9 %copy-done.3 = f32[256,256]{1,0:T(8,128)S(1)} copy-done((f32[256,256]{1,0:T(8,128)S(1)}, f32[256,256]{1,0:T(8,128)}, u32[]{:S(2)}) %copy-start.3) | copy-done | bytes 262168
  5.3 0.0 copy-start.6
  5.3 0.7 copy-done.6
  6.0 68.6 %shard_map.103 = (f32[512,256]{1,0:T(8,128)S(1)}, f32[256,256]{1,0:T(8,128)S(1)}, f32[256,256]{1,0:T(8,128)S(1)}) custom-call(f32[512,256]{1,0:T(8,128)S(1)} %copy-done, s32[4,128]{1,0:T(4,128)S(1)} %bitcast.3, f32[256,256]{1,0:T(8,128)S(1)} %copy-done.2, f32[256,256]{1,0:T(8,128)S(1)} %copy-done.3, f32[512,256]{1,0:T(8,128)S(1)} %copy-done.1, ...), custom_call_target="tpu_custom_call" | custom-call | tf_op jit(solution)/shard_map/pallas_call | solution.py:248
  74.6 0.8 %copy.14 = f32[512,256]{1,0:T(8,128)} copy(f32[512,256]{1,0:T(8,128)S(1)} %get-tuple-element.6) | data formatting | bytes 1048576
  75.4 0.7 copy.15
  76.1 0.7 copy.16
Async XLA Ops:
  0.6 0.7 copy-start.5
  0.6 0.7 copy-start.4
  0.7 0.7 copy-start.7
  1.3 1.0 %copy-start = (f32[512,256]{1,0:T(8,128)S(1)}, f32[512,256]{1,0:T(8,128)}, u32[]{:S(2)}) copy-start(f32[512,256]{1,0:T(8,128)} %features.1) | copy-start | bytes 1572868
  2.4 1.0 %copy-start.1 = (f32[512,256]{1,0:T(8,128)S(1)}, f32[512,256]{1,0:T(8,128)}, u32[]{:S(2)}) copy-start(f32[512,256]{1,0:T(8,128)} %cotangent.1) | copy-start | bytes 1572868
  3.4 0.9 %copy-start.2 = (f32[256,256]{1,0:T(8,128)S(1)}, f32[256,256]{1,0:T(8,128)}, u32[]{:S(2)}) copy-start(f32[256,256]{1,0:T(8,128)} %theta_one.1) | copy-start | bytes 786436
  4.4 0.9 %copy-start.3 = (f32[256,256]{1,0:T(8,128)S(1)}, f32[256,256]{1,0:T(8,128)}, u32[]{:S(2)}) copy-start(f32[256,256]{1,0:T(8,128)} %theta_two.1) | copy-start | bytes 786436
  5.3 0.7 copy-start.6
where the time goes:
time: 77.1 us; the launch traced here: 76.8 us
  Pallas kernels  68.6 us (89%)
  local copies, waits for them, and re-layouts  7.54 us (10%)
    pallas_call x1, Pallas kernels, body(): pl.pallas_call(functools.partial(kernel, n, slots), out_shape=(jax.ShapeD...  68.6 us
    unnamed x19, local copies, waits for them, and re-layouts  7.54 us

commit v1 on v0

--- a/solution.py
+++ b/solution.py
@@ -9,8 +9,26 @@
 
 MESH = pl.DeviceIdType.MESH
 F32, BF16 = jnp.float32, jnp.bfloat16
-UNROLL = 8
+ROW = 8
 A_DOWN, B_DOWN, A_UP, B_UP, C_DOWN, C_UP, PAIR_IN, SCATTER, GATHER, PAIR_OUT = range(10)
+
+
+SIDE = 4
+
+
+def far_first():
+    left = [(z, x, y) for z in range(SIDE) for x in range(SIDE) for y in range(SIDE)][1:]
+    runs = []
+    while left:
+        z, x, y = left[0]
+        run = []
+        for step in ((z, x, y), (x, y, z), (y, z, x)):
+            for there in (step, tuple(-v % SIDE for v in step)):
+                if there not in run:
+                    run.append(there)
+        left = [there for there in left if there not in run]
+        runs.append(run)
+    return sorted(runs, key=lambda run: -sum(min(v, SIDE - v) for v in run[0]))
 
 
 def split(x):
@@ -34,32 +52,48 @@
 
 
 def kernel(
-    n, slots, features, keep, theta_one, theta_two, cotangent, send_node, recv_edge, send_count,
-    grad_features, grad_one, grad_two,
-    gather, spread, meet, out, back, terms, partner, pair_sum, parts, total, send_sem, recv_sem,
+    n, slots, *refs,
 ):
+    given, (grad_features, grad_one, grad_two), held = refs[:8], refs[8:11], refs[11:19]
+    (
+        gather, spread, meet, out, back, terms, partner, pair_sum, parts, total, send_sem, recv_sem, load_sem,
+        row_ready,
+    ) = refs[19:]
+    features, keep, theta_one, theta_two, cotangent, send_node, recv_edge, send_count = held
+    loads = [pltpu.make_async_copy(given[i], held[i], load_sem.at[i]) for i in range(8)]
+    for i in (5, 7, 6, 1, 0, 4, 2, 3):
+        loads[i].start()
     me = lax.axis_index("dev")
     core, chip, chips = lax.rem(me, 2), me // 2, n // 2
     other = me + 1 - 2 * core
+    place = (me // (2 * SIDE * SIDE), lax.rem(me // (2 * SIDE), SIDE), lax.rem(chip, SIDE))
+    along = [
+        [lax.rem(place[axis] + v, SIDE) * pitch for v in range(SIDE)]
+        for axis, pitch in enumerate((2 * SIDE * SIDE, 2 * SIDE, 2))
+    ]
+    cores = (core, 1 - core)
+
+    def peers(which):
+        for run in far_first():
+            for c in which:
+                for z, x, y in run:
+                    yield along[0][z] + along[1][x] + along[2][y] + c
     nodes, width = features.shape
     lanes = width // 2
     tile = 2 * slots
 
     barrier = pltpu.get_barrier_semaphore()
-
-    def greet(_, peer):
-        peer = lax.rem(peer + 1, n)
+    row, column, rows, columns = me // ROW, lax.rem(me, ROW), n // ROW, ROW
+    in_row = [row * columns + lax.rem(column + k, columns) for k in range(1, columns)]
+    in_column = [lax.rem(row + k, rows) * columns + column for k in range(1, rows)]
+    for peer in in_row + in_column:
         pl.semaphore_signal(barrier, inc=1, device_id=(peer,), device_id_type=MESH)
-        return peer
-
-    lax.fori_loop(0, n - 1, greet, me, unroll=UNROLL)
 
     def block(index, rows=tile):
         return pl.ds(pl.multiple_of(index * rows, rows), rows)
 
     def exchange(phase, src, dst):
-        def push(_, peer):
-            peer = lax.rem(peer + 1, n)
+        for peer in [*peers(cores), other]:
             pltpu.make_async_remote_copy(
                 src_ref=src.at[block(peer)],
                 dst_ref=dst.at[block(me)],
@@ -68,14 +102,10 @@
                 device_id=(peer,),
                 device_id_type=MESH,
             ).start()
-            return peer
-
-        lax.fori_loop(0, n - 1, push, me, unroll=UNROLL)
         pltpu.make_async_copy(src.at[block(me)], dst.at[block(me)], recv_sem.at[phase]).start()
 
     def chip_exchange(phase, src_block, dst):
-        def push(_, peer):
-            peer = lax.rem(peer + 2, n)
+        for peer in peers((core,)):
             pltpu.make_async_remote_copy(
                 src_ref=src_block(peer // 2),
                 dst_ref=dst.at[block(chip)],
@@ -84,9 +114,6 @@
                 device_id=(peer,),
                 device_id_type=MESH,
             ).start()
-            return peer
-
-        lax.fori_loop(0, chips - 1, push, me, unroll=UNROLL)
         pltpu.make_async_copy(src_block(chip), dst.at[block(chip)], recv_sem.at[phase]).start()
 
     def arrived(phase, ref):
@@ -113,6 +140,12 @@
     def as_column(row):
         return jnp.sum(jnp.where(eye, row, 0.0), axis=1, keepdims=True)
 
+    pl.semaphore_wait(barrier, rows + columns - 2)
+    for peer in in_column:
+        pl.semaphore_signal(row_ready, inc=1, device_id=(peer,), device_id_type=MESH)
+
+    for i in (5, 7, 6, 1):
+        loads[i].wait()
     count = send_count[...].astype(F32)
     node_of = send_node[0].astype(F32)
     edge_of = recv_edge[0].astype(F32)
@@ -143,10 +176,12 @@
             part = rows[j * n : (j + 1) * n]
             put(ref, j, jnp.where(live[j], part, jnp.inf) if mark else part)
 
+    loads[0].wait()
     load_out(out.at[A_DOWN], features[...] * keep_f, True)
-    pl.semaphore_wait(barrier, n - 1)
+    loads[4].wait()
+    load_out(out.at[B_DOWN], cotangent[...], False)
+    pl.semaphore_wait(row_ready, rows - 1)
     exchange(A_DOWN, out.at[A_DOWN], back.at[A_DOWN])
-    load_out(out.at[B_DOWN], cotangent[...], False)
     exchange(B_DOWN, out.at[B_DOWN], back.at[B_DOWN])
 
     arrived(A_DOWN, back.at[A_DOWN])
@@ -175,6 +210,8 @@
 
     arrived(A_UP, back.at[A_UP])
     spread_in = pick(spread[...], take(back.at[A_UP])) * node_scale
+    loads[2].wait()
+    loads[3].wait()
     pre = matmul(spread_in, theta_one[...])
     grow = jnp.exp(jnp.minimum(pre, 0.0))
     hidden = jnp.where(pre > 0, pre, grow - 1.0)
@@ -237,6 +274,14 @@
             ref[:, h * lanes : (h + 1) * lanes] = total[k, h * width : (h + 1) * width, :]
 
 
+def write_out(*refs):
+    copies = [pltpu.make_async_copy(refs[i], refs[3 + i], refs[6].at[i]) for i in range(3)]
+    for copy in copies:
+        copy.start()
+    for copy in copies:
+        copy.wait()
+
+
 def solution(mesh):
     n = mesh.shape["dev"]
 
@@ -245,16 +290,22 @@
         slots = send_node.shape[2]
         rows = n * 2 * slots
         whole = pl.BlockSpec(memory_space=pltpu.VMEM)
-        return pl.pallas_call(
+        given = (
+            features, keep.reshape(nodes // n, n), theta_one, theta_two, cotangent,
+            send_node.transpose(0, 2, 1), recv_edge.transpose(0, 2, 1), send_count,
+        )
+        given = [pltpu.with_memory_space_constraint(x, pltpu.HBM) for x in given]
+        results = pl.pallas_call(
             functools.partial(kernel, n, slots),
             out_shape=(
                 jax.ShapeDtypeStruct((nodes, width), F32),
                 jax.ShapeDtypeStruct((width, width), F32),
                 jax.ShapeDtypeStruct((width, width), F32),
             ),
-            in_specs=[whole] * 8,
+            in_specs=[pl.BlockSpec(memory_space=pltpu.HBM)] * 8,
             out_specs=(whole,) * 3,
-            scratch_shapes=[
+            scratch_shapes=[pltpu.VMEM(x.shape, x.dtype) for x in given]
+            + [
                 pltpu.VMEM((slots * n, nodes), BF16),
                 pltpu.VMEM((nodes, slots * n), BF16),
                 pltpu.VMEM((slots * n, slots * n), BF16),
@@ -267,14 +318,21 @@
                 pltpu.VMEM((2, 2 * width, width // 2), F32),
                 pltpu.SemaphoreType.DMA((10,)),
                 pltpu.SemaphoreType.DMA((10,)),
+                pltpu.SemaphoreType.DMA((8,)),
+                pltpu.SemaphoreType.REGULAR,
             ],
             compiler_params=pltpu.CompilerParams(
                 collective_id=0, has_side_effects=True, vmem_limit_bytes=48 << 20
             ),
-        )(
-            features, keep.reshape(nodes // n, n), theta_one, theta_two, cotangent,
-            send_node.transpose(0, 2, 1), recv_edge.transpose(0, 2, 1), send_count,
-        )
+        )(*given)
+        return pl.pallas_call(
+            write_out,
+            out_shape=tuple(jax.ShapeDtypeStruct(x.shape, x.dtype) for x in results),
+            in_specs=[whole] * 3,
+            out_specs=(pl.BlockSpec(memory_space=pltpu.HBM),) * 3,
+            scratch_shapes=[pltpu.SemaphoreType.DMA((3,))],
+            compiler_params=pltpu.CompilerParams(vmem_limit_bytes=8 << 20),
+        )(*[pltpu.with_memory_space_constraint(x, pltpu.VMEM) for x in results])
 
     placed = (
         P("dev", None),

time: 77.1 us -> 67.2 us (0.87)
  local copies, waits for them, and re-layouts: 7.54 us -> 0 us
  Pallas kernels: 68.6 us -> 66.4 us
    unnamed x19 -> x0, local copies, waits for them, and re-layouts: 7.54 us -> none
    pallas_call x1, Pallas kernels: 68.6 us -> 65.4 us  [body(): pl.pallas_call(functools.partial(kernel, n, slots), out_shape=(jax.ShapeD...]
    pallas_call x0 -> x1, Pallas kernels: none -> 0.99 us  [body(): pl.pallas_call(write_out, out_shape=tuple((jax.ShapeDtypeStruct(x.shape,...]
where the time goes in v1:
time: 67.2 us; the launch traced here: 67 us
  Pallas kernels  66.4 us (99%)
    pallas_call x1, Pallas kernels, body(): pl.pallas_call(functools.partial(kernel, n, slots), out_shape=(jax.ShapeD...  65.4 us

profile of v1, /device:TPU:1, one launch (start us, length us, event | category | flops | bytes accessed | tf_op | source)
XLA Modules:
  0.0 67.0 jit_solution(7308697787371303923)
XLA Ops:
  0.6 65.4 %shard_map.103 = (f32[512,256]{1,0:T(8,128)S(1)}, f32[256,256]{1,0:T(8,128)S(1)}, f32[256,256]{1,0:T(8,128)S(1)}) custom-call(f32[512,256]{1,0:T(8,128)} %refs_0_.1, s32[4,128]{1,0:T(4,128)} %bitcast.3, f32[256,256]{1,0:T(8,128)} %refs_2_.1, f32[256,256]{1,0:T(8,128)} %refs_3_.1, f32[512,256]{1,0:T(8,128)} %refs_4_.1, s32[1,4,128]{2,1,0:T(4,128)} %bitcast.4, ...), custom_call_target="tpu_custom_call" | custom-call | tf_op jit(solution)/shard_map/pallas_call | solution.py:298
  66.1 1.0 %shard_map.104 = (f32[512,256]{1,0:T(8,128)}, f32[256,256]{1,0:T(8,128)}, f32[256,256]{1,0:T(8,128)}) custom-call(f32[512,256]{1,0:T(8,128)S(1)} %get-tuple-element.6.refs_0_, f32[256,256]{1,0:T(8,128)S(1)} %get-tuple-element.7.refs_1_, f32[256,256]{1,0:T(8,128)S(1)} %get-tuple-element.8.refs_2_), custom_call_target="tpu_custom_call" | custom-call | tf_op jit(solution)/shard_map/pallas_call | solution.py:328

commit v2 on v1

--- a/solution.py
+++ b/solution.py
@@ -9,8 +9,9 @@
 
 MESH = pl.DeviceIdType.MESH
 F32, BF16 = jnp.float32, jnp.bfloat16
-ROW = 8
-A_DOWN, B_DOWN, A_UP, B_UP, C_DOWN, C_UP, PAIR_IN, SCATTER, GATHER, PAIR_OUT = range(10)
+PAIR_IN, SCATTER, GATHER, PAIR_OUT = range(4)
+UNITS_A, UNITS_B, UNITS_C = ((0,), (1,)), ((0,), (1,)), ((0,), (1,))
+UNITS = UNITS_A + UNITS_B + UNITS_C
 
 
 SIDE = 4
@@ -56,8 +57,7 @@
 ):
     given, (grad_features, grad_one, grad_two), held = refs[:8], refs[8:11], refs[11:19]
     (
-        gather, spread, meet, out, back, terms, partner, pair_sum, parts, total, send_sem, recv_sem, load_sem,
-        row_ready,
+        gather, spread, meet, terms, partner, pair_sum, parts, total, send_sem, recv_sem, load_sem, *boxes,
     ) = refs[19:]
     features, keep, theta_one, theta_two, cotangent, send_node, recv_edge, send_count = held
     loads = [pltpu.make_async_copy(given[i], held[i], load_sem.at[i]) for i in range(8)]
@@ -83,10 +83,7 @@
     tile = 2 * slots
 
     barrier = pltpu.get_barrier_semaphore()
-    row, column, rows, columns = me // ROW, lax.rem(me, ROW), n // ROW, ROW
-    in_row = [row * columns + lax.rem(column + k, columns) for k in range(1, columns)]
-    in_column = [lax.rem(row + k, rows) * columns + column for k in range(1, rows)]
-    for peer in in_row + in_column:
+    for peer in [*peers(cores), other]:
         pl.semaphore_signal(barrier, inc=1, device_id=(peer,), device_id_type=MESH)
 
     def block(index, rows=tile):
@@ -95,14 +92,14 @@
     def exchange(phase, src, dst):
         for peer in [*peers(cores), other]:
             pltpu.make_async_remote_copy(
-                src_ref=src.at[block(peer)],
-                dst_ref=dst.at[block(me)],
+                src_ref=src.at[peer],
+                dst_ref=dst.at[me],
                 send_sem=send_sem.at[phase],
                 recv_sem=recv_sem.at[phase],
                 device_id=(peer,),
                 device_id_type=MESH,
             ).start()
-        pltpu.make_async_copy(src.at[block(me)], dst.at[block(me)], recv_sem.at[phase]).start()
+        pltpu.make_async_copy(src.at[me], dst.at[me], recv_sem.at[phase]).start()
 
     def chip_exchange(phase, src_block, dst):
         for peer in peers((core,)):
@@ -122,16 +119,23 @@
     def sent(phase, ref):
         pltpu.make_async_copy(ref, ref, send_sem.at[phase]).wait()
 
+    down, there, up, here_again = (boxes[k :: 4] for k in range(4))
+    first_b, first_c = len(UNITS_A), len(UNITS_A) + len(UNITS_B)
+    units_a, units_b, units_c = range(first_b), range(first_b, first_c), range(first_c, len(UNITS))
+
     def put(ref, j, rows):
-        for h in range(2):
-            ref[pl.ds(h * slots + j, n, stride=tile), :] = rows[:, h * lanes : (h + 1) * lanes]
+        for h in range(rows.shape[1] // lanes):
+            ref[:, h * slots + j, :] = rows[:, h * lanes : (h + 1) * lanes]
 
     def get(ref, j):
-        return [ref[pl.ds(h * slots + j, n, stride=tile), :] for h in range(2)]
+        return [ref[:, h * slots + j, :] for h in range(ref.shape[1] // slots)]
 
     def take(ref):
         return jnp.concatenate([jnp.concatenate(get(ref, j), axis=1) for j in range(slots)], axis=0)
 
+    def columns(x, u):
+        return x[:, UNITS[u][0] * lanes : (UNITS[u][-1] + 1) * lanes]
+
     eye = lax.broadcasted_iota(jnp.int32, (n, n), 0) == lax.broadcasted_iota(jnp.int32, (n, n), 1)
 
     def as_row(column):
@@ -139,10 +143,6 @@
 
     def as_column(row):
         return jnp.sum(jnp.where(eye, row, 0.0), axis=1, keepdims=True)
-
-    pl.semaphore_wait(barrier, rows + columns - 2)
-    for peer in in_column:
-        pl.semaphore_signal(row_ready, inc=1, device_id=(peer,), device_id_type=MESH)
 
     for i in (5, 7, 6, 1):
         loads[i].wait()
@@ -170,63 +170,82 @@
     keep_rows = keep[...].astype(F32)
     keep_f = jnp.concatenate([as_column(keep_rows[r : r + 1]) for r in range(nodes // n)], axis=0)
 
-    def load_out(ref, field, mark):
-        rows = pick(gather[...], field * node_scale)
+    def load_out(u, field):
+        rows = pick(gather[...], columns(field, u) * node_scale)
         for j in range(slots):
             part = rows[j * n : (j + 1) * n]
-            put(ref, j, jnp.where(live[j], part, jnp.inf) if mark else part)
+            put(down[u], j, jnp.where(live[j], part, jnp.inf) if u == 0 else part)
+
+    def send_down(u):
+        exchange(2 * u + 4, down[u], there[u])
+
+    def send_up(u):
+        exchange(2 * u + 5, up[u], here_again[u])
 
     loads[0].wait()
-    load_out(out.at[A_DOWN], features[...] * keep_f, True)
+    dropped = features[...] * keep_f
+    for u in units_a:
+        load_out(u, dropped)
     loads[4].wait()
-    load_out(out.at[B_DOWN], cotangent[...], False)
-    pl.semaphore_wait(row_ready, rows - 1)
-    exchange(A_DOWN, out.at[A_DOWN], back.at[A_DOWN])
-    exchange(B_DOWN, out.at[B_DOWN], back.at[B_DOWN])
-
-    arrived(A_DOWN, back.at[A_DOWN])
-    fields, alive = [], []
-    for j in range(slots):
-        halves = get(back.at[A_DOWN], j)
-        is_live = halves[0][:, :1] < jnp.inf
-        alive.append(is_live.astype(F32))
-        fields.append(jnp.where(is_live, jnp.concatenate(halves, axis=1), 0.0))
-    alive_row = jnp.concatenate([as_row(a) for a in alive], axis=1)
-    edge_scale = []
-    for j in range(slots):
-        shared = jnp.where(edge_row == edge_cols[j], alive_row, 0.0)
-        edge_scale.append(1.0 / jnp.maximum(jnp.sum(shared, axis=1, keepdims=True), 1.0))
-
-    def load_back(ref, field):
+    for u in units_b:
+        load_out(u, cotangent[...])
+    pl.semaphore_wait(barrier, n - 1)
+    for u in (*units_a, *units_b):
+        send_down(u)
+
+    def load_up(u, field):
         rows = pick(meet[...], field)
         for j in range(slots):
-            put(ref, j, rows[j * n : (j + 1) * n] * edge_scale[j])
-
-    load_back(out.at[A_UP], jnp.concatenate(fields, axis=0))
-    exchange(A_UP, out.at[A_UP], back.at[A_UP])
-    arrived(B_DOWN, back.at[B_DOWN])
-    load_back(out.at[B_UP], take(back.at[B_DOWN]))
-    exchange(B_UP, out.at[B_UP], back.at[B_UP])
-
-    arrived(A_UP, back.at[A_UP])
-    spread_in = pick(spread[...], take(back.at[A_UP])) * node_scale
+            put(up[u], j, rows[j * n : (j + 1) * n] * edge_scale[j])
+
+    edge_scale = []
+    for u in (*units_a, *units_b):
+        arrived(2 * u + 4, there[u])
+        if u == 0:
+            fields, alive = [], []
+            for j in range(slots):
+                pieces = get(there[u], j)
+                is_live = pieces[0][:, :1] < jnp.inf
+                alive.append(is_live.astype(F32))
+                fields.append(jnp.where(is_live, jnp.concatenate(pieces, axis=1), 0.0))
+            field = jnp.concatenate(fields, axis=0)
+            alive_row = jnp.concatenate([as_row(a) for a in alive], axis=1)
+            for j in range(slots):
+                shared = jnp.where(edge_row == edge_cols[j], alive_row, 0.0)
+                edge_scale.append(1.0 / jnp.maximum(jnp.sum(shared, axis=1, keepdims=True), 1.0))
+        else:
+            field = take(there[u])
+        load_up(u, field)
+        send_up(u)
+
+    def propagated(u):
+        arrived(2 * u + 5, here_again[u])
+        return pick(spread[...], take(here_again[u])) * node_scale
+
+    def set_term(k, halves, term):
+        for i, h in enumerate(halves):
+            terms[k, h * width : (h + 1) * width, :] = term[:, i * lanes : (i + 1) * lanes]
+
+    spread_in = jnp.concatenate([propagated(u) for u in units_a], axis=1)
     loads[2].wait()
     loads[3].wait()
     pre = matmul(spread_in, theta_one[...])
     grow = jnp.exp(jnp.minimum(pre, 0.0))
     hidden = jnp.where(pre > 0, pre, grow - 1.0)
     slope = jnp.where(pre > 0, 1.0, grow)
-    arrived(B_UP, back.at[B_UP])
-    spread_cot = pick(spread[...], take(back.at[B_UP])) * node_scale
-    grad_pre = matmul(spread_cot, theta_two[...], ((1,), (1,))) * slope
-    load_out(out.at[C_DOWN], grad_pre, False)
-    exchange(C_DOWN, out.at[C_DOWN], back.at[C_DOWN])
-
-    term_one = matmul(spread_in, grad_pre, ((0,), (0,)))
-    term_two = matmul(hidden, spread_cot, ((0,), (0,)))
-    for k, term in enumerate((term_one, term_two)):
-        for h in range(2):
-            terms[k, h * width : (h + 1) * width, :] = term[:, h * lanes : (h + 1) * lanes]
+    hidden_t, spread_in_t = hidden.T, spread_in.T
+    pulled = 0.0
+    for u in units_b:
+        spread_cot = propagated(u)
+        pulled += matmul(spread_cot, columns(theta_two[...], u), ((1,), (1,)))
+        if u != units_b[-1]:
+            set_term(1, UNITS[u], matmul(hidden_t, spread_cot))
+    grad_pre = pulled * slope
+    load_out(units_c[0], grad_pre)
+    send_down(units_c[0])
+
+    set_term(1, UNITS[units_b[-1]], matmul(hidden_t, spread_cot))
+    set_term(0, (0, 1), matmul(spread_in_t, grad_pre))
     pltpu.make_async_remote_copy(
         src_ref=terms.at[1 - core],
         dst_ref=partner,
@@ -235,13 +254,17 @@
         device_id=(other,),
         device_id_type=MESH,
     ).start()
+    for u in units_c[1:]:
+        load_out(u, grad_pre)
+        send_down(u)
     arrived(PAIR_IN, partner)
     pair_sum[...] = terms[core] + partner[...]
     chip_exchange(SCATTER, lambda q: pair_sum.at[block(q)], parts)
 
-    arrived(C_DOWN, back.at[C_DOWN])
-    load_back(out.at[C_UP], take(back.at[C_DOWN]))
-    exchange(C_UP, out.at[C_UP], back.at[C_UP])
+    for u in units_c:
+        arrived(2 * u + 4, there[u])
+        load_up(u, take(there[u]))
+        send_up(u)
 
     arrived(SCATTER, parts)
     sent(SCATTER, parts.at[pl.ds(0, (chips - 1) * tile)])
@@ -250,9 +273,10 @@
     pair_sum[:tile, :] = summed
     chip_exchange(GATHER, lambda q: pair_sum.at[pl.ds(0, tile)], total.at[core])
 
-    arrived(C_UP, back.at[C_UP])
-    spread_grad = pick(spread[...], take(back.at[C_UP])) * node_scale
-    grad_features[...] = matmul(spread_grad, theta_one[...], ((1,), (1,))) * keep_f
+    pulled = 0.0
+    for u in units_c:
+        pulled += matmul(propagated(u), columns(theta_one[...], u), ((1,), (1,)))
+    grad_features[...] = pulled * keep_f
 
     arrived(GATHER, total.at[core])
     pltpu.make_async_remote_copy(
@@ -263,8 +287,9 @@
         device_id=(other,),
         device_id_type=MESH,
     ).start()
-    for phase in (A_DOWN, B_DOWN, A_UP, B_UP, C_DOWN, C_UP):
-        sent(phase, out.at[phase, pl.ds(0, (n - 1) * tile)])
+    for u in range(len(UNITS)):
+        sent(2 * u + 4, down[u].at[pl.ds(0, n - 1)])
+        sent(2 * u + 5, up[u].at[pl.ds(0, n - 1)])
     sent(PAIR_IN, partner)
     sent(GATHER, parts.at[pl.ds(0, (chips - 1) * tile)])
     sent(PAIR_OUT, partner)
@@ -288,7 +313,6 @@
     def body(features, keep, theta_one, theta_two, cotangent, send_node, recv_edge, send_count):
         nodes, width = features.shape
         slots = send_node.shape[2]
-        rows = n * 2 * slots
         whole = pl.BlockSpec(memory_space=pltpu.VMEM)
         given = (
             features, keep.reshape(nodes // n, n), theta_one, theta_two, cotangent,
@@ -309,18 +333,16 @@
                 pltpu.VMEM((slots * n, nodes), BF16),
                 pltpu.VMEM((nodes, slots * n), BF16),
                 pltpu.VMEM((slots * n, slots * n), BF16),
-                pltpu.VMEM((6, rows, width // 2), F32),
-                pltpu.VMEM((6, rows, width // 2), F32),
                 pltpu.VMEM((2, 2 * width, width // 2), F32),
                 pltpu.VMEM((2 * width, width // 2), F32),
                 pltpu.VMEM((2 * width, width // 2), F32),
                 pltpu.VMEM((2 * width, width // 2), F32),
                 pltpu.VMEM((2, 2 * width, width // 2), F32),
-                pltpu.SemaphoreType.DMA((10,)),
-                pltpu.SemaphoreType.DMA((10,)),
+                pltpu.SemaphoreType.DMA((4 + 2 * len(UNITS),)),
+                pltpu.SemaphoreType.DMA((4 + 2 * len(UNITS),)),
                 pltpu.SemaphoreType.DMA((8,)),
-                pltpu.SemaphoreType.REGULAR,
-            ],
+            ]
+            + [pltpu.VMEM((n, len(unit) * slots, width // 2), F32) for unit in UNITS for _ in range(4)],
             compiler_params=pltpu.CompilerParams(
                 collective_id=0, has_side_effects=True, vmem_limit_bytes=48 << 20
             ),

time: 67.2 us -> 63.2 us (0.940)
  Pallas kernels: 66.4 us -> 62.3 us
    pallas_call x1, Pallas kernels: 65.4 us -> 61.3 us  [body(): pl.pallas_call(functools.partial(kernel, n, slots), out_shape=(jax.ShapeD...]
where the time goes in v2:
time: 63.2 us; the launch traced here: 63.1 us
  Pallas kernels  62.3 us (99%)
  between operations  0.8 us (1%)
    pallas_call x1, Pallas kernels, body(): pl.pallas_call(functools.partial(kernel, n, slots), out_shape=(jax.ShapeD...  61.3 us

profile of v2, /device:TPU:1, one launch (start us, length us, event | category | flops | bytes accessed | tf_op | source)
XLA Modules:
  0.0 63.1 jit_solution(15496944411195884014)
XLA Ops:
  0.6 61.3 %shard_map.103 = (f32[512,256]{1,0:T(8,128)S(1)}, f32[256,256]{1,0:T(8,128)S(1)}, f32[256,256]{1,0:T(8,128)S(1)}) custom-call(f32[512,256]{1,0:T(8,128)} %refs_0_.1, s32[4,128]{1,0:T(4,128)} %bitcast.3, f32[256,256]{1,0:T(8,128)} %refs_2_.1, f32[256,256]{1,0:T(8,128)} %refs_3_.1, f32[512,256]{1,0:T(8,128)} %refs_4_.1, s32[1,4,128]{2,1,0:T(4,128)} %bitcast.4, ...), custom_call_target="tpu_custom_call" | custom-call | tf_op jit(solution)/shard_map/pallas_call | solution.py:322
  61.9 1.0 %shard_map.104 = (f32[512,256]{1,0:T(8,128)}, f32[256,256]{1,0:T(8,128)}, f32[256,256]{1,0:T(8,128)}) custom-call(f32[512,256]{1,0:T(8,128)S(1)} %get-tuple-element.6.refs_0_, f32[256,256]{1,0:T(8,128)S(1)} %get-tuple-element.7.refs_1_, f32[256,256]{1,0:T(8,128)S(1)} %get-tuple-element.8.refs_2_), custom_call_target="tpu_custom_call" | custom-call | tf_op jit(solution)/shard_map/pallas_call | solution.py:350

commit v3 on v2

--- a/solution.py
+++ b/solution.py
@@ -47,8 +47,7 @@
 
 
 def matmul(left, right, dims=((1,), (0,))):
-    lh, ll = split(left)
-    rh, rl = split(right)
+    (lh, ll), (rh, rl) = left, right
     return dot(lh, rh, dims) + (dot(lh, rl, dims) + dot(ll, rh, dims))
 
 
@@ -61,7 +60,7 @@
     ) = refs[19:]
     features, keep, theta_one, theta_two, cotangent, send_node, recv_edge, send_count = held
     loads = [pltpu.make_async_copy(given[i], held[i], load_sem.at[i]) for i in range(8)]
-    for i in (5, 7, 6, 1, 0, 4, 2, 3):
+    for i in (5, 7, 1):
         loads[i].start()
     me = lax.axis_index("dev")
     core, chip, chips = lax.rem(me, 2), me // 2, n // 2
@@ -85,6 +84,8 @@
     barrier = pltpu.get_barrier_semaphore()
     for peer in [*peers(cores), other]:
         pl.semaphore_signal(barrier, inc=1, device_id=(peer,), device_id_type=MESH)
+    for i in (0, 4, 6, 2, 3):
+        loads[i].start()
 
     def block(index, rows=tile):
         return pl.ds(pl.multiple_of(index * rows, rows), rows)
@@ -144,11 +145,10 @@
     def as_column(row):
         return jnp.sum(jnp.where(eye, row, 0.0), axis=1, keepdims=True)
 
-    for i in (5, 7, 6, 1):
+    for i in (5, 7, 1):
         loads[i].wait()
     count = send_count[...].astype(F32)
     node_of = send_node[0].astype(F32)
-    edge_of = recv_edge[0].astype(F32)
     node_lane = lax.broadcasted_iota(jnp.int32, (n, nodes), 1).astype(F32)
     node_row = lax.broadcasted_iota(jnp.int32, (nodes, n), 0).astype(F32)
     degree = jnp.zeros((nodes, n), F32)
@@ -161,10 +161,6 @@
         here = (node_row == mine).astype(F32)
         degree += here
         spread[:, j * n : (j + 1) * n] = here.astype(BF16)
-    edge_cols = [as_column(edge_of[j : j + 1]) for j in range(slots)]
-    edge_row = jnp.concatenate([edge_of[j : j + 1] for j in range(slots)], axis=1)
-    for j in range(slots):
-        meet[j * n : (j + 1) * n, :] = (edge_row == edge_cols[j]).astype(F32).astype(BF16)
     degree = jnp.sum(degree, axis=1, keepdims=True)
     node_scale = 1.0 / jnp.sqrt(jnp.maximum(degree, 1.0))
     keep_rows = keep[...].astype(F32)
@@ -186,12 +182,24 @@
     dropped = features[...] * keep_f
     for u in units_a:
         load_out(u, dropped)
+    pl.semaphore_wait(barrier, n - 1)
+    for u in units_a:
+        send_down(u)
     loads[4].wait()
     for u in units_b:
         load_out(u, cotangent[...])
-    pl.semaphore_wait(barrier, n - 1)
-    for u in (*units_a, *units_b):
         send_down(u)
+
+    loads[6].wait()
+    edge_of = recv_edge[0].astype(F32)
+    edge_cols = [as_column(edge_of[j : j + 1]) for j in range(slots)]
+    edge_row = jnp.concatenate([edge_of[j : j + 1] for j in range(slots)], axis=1)
+    for j in range(slots):
+        meet[j * n : (j + 1) * n, :] = (edge_row == edge_cols[j]).astype(F32).astype(BF16)
+    loads[2].wait()
+    loads[3].wait()
+    theta_one_split = split(theta_one[...])
+    theta_two_split = split(theta_two[...])
 
     def load_up(u, field):
         rows = pick(meet[...], field)
@@ -227,17 +235,19 @@
             terms[k, h * width : (h + 1) * width, :] = term[:, i * lanes : (i + 1) * lanes]
 
     spread_in = jnp.concatenate([propagated(u) for u in units_a], axis=1)
-    loads[2].wait()
-    loads[3].wait()
-    pre = matmul(spread_in, theta_one[...])
-    grow = jnp.exp(jnp.minimum(pre, 0.0))
-    hidden = jnp.where(pre > 0, pre, grow - 1.0)
+    pre = matmul(split(spread_in), theta_one_split)
+    below = jnp.minimum(pre, 0.0)
+    grow = jnp.exp(below)
+    series = 1.0 + below / 7
+    for k in (6, 5, 4, 3, 2):
+        series = 1.0 + below * series * (1.0 / k)
+    hidden = jnp.where(pre > 0, pre, jnp.where(below > -0.25, below * series, grow - 1.0))
     slope = jnp.where(pre > 0, 1.0, grow)
-    hidden_t, spread_in_t = hidden.T, spread_in.T
+    hidden_t, spread_in_t = split(hidden.T), split(spread_in.T)
     pulled = 0.0
     for u in units_b:
-        spread_cot = propagated(u)
-        pulled += matmul(spread_cot, columns(theta_two[...], u), ((1,), (1,)))
+        spread_cot = split(propagated(u))
+        pulled += matmul(spread_cot, [columns(x, u) for x in theta_two_split], ((1,), (1,)))
         if u != units_b[-1]:
             set_term(1, UNITS[u], matmul(hidden_t, spread_cot))
     grad_pre = pulled * slope
@@ -245,7 +255,7 @@
     send_down(units_c[0])
 
     set_term(1, UNITS[units_b[-1]], matmul(hidden_t, spread_cot))
-    set_term(0, (0, 1), matmul(spread_in_t, grad_pre))
+    set_term(0, (0, 1), matmul(spread_in_t, split(grad_pre)))
     pltpu.make_async_remote_copy(
         src_ref=terms.at[1 - core],
         dst_ref=partner,
@@ -275,7 +285,7 @@
 
     pulled = 0.0
     for u in units_c:
-        pulled += matmul(propagated(u), columns(theta_one[...], u), ((1,), (1,)))
+        pulled += matmul(split(propagated(u)), [columns(x, u) for x in theta_one_split], ((1,), (1,)))
     grad_features[...] = pulled * keep_f
 
     arrived(GATHER, total.at[core])

time: 63.2 us -> 63.2 us (level)
  no operation moved by 1% of the time
where the time goes in v3:
time: 63.2 us; the launch traced here: 63.1 us
  Pallas kernels  62.3 us (99%)
  between operations  0.8 us (1%)
    pallas_call x1, Pallas kernels, body(): pl.pallas_call(functools.partial(kernel, n, slots), out_shape=(jax.ShapeD...  61.3 us

profile of v3, /device:TPU:1, one launch (start us, length us, event | category | flops | bytes accessed | tf_op | source)
XLA Modules:
  0.0 63.1 jit_solution(17165704090250510709)
XLA Ops:
  0.6 61.3 %shard_map.103 = (f32[512,256]{1,0:T(8,128)S(1)}, f32[256,256]{1,0:T(8,128)S(1)}, f32[256,256]{1,0:T(8,128)S(1)}) custom-call(f32[512,256]{1,0:T(8,128)} %refs_0_.1, s32[4,128]{1,0:T(4,128)} %bitcast.3, f32[256,256]{1,0:T(8,128)} %refs_2_.1, f32[256,256]{1,0:T(8,128)} %refs_3_.1, f32[512,256]{1,0:T(8,128)} %refs_4_.1, s32[1,4,128]{2,1,0:T(4,128)} %bitcast.4, ...), custom_call_target="tpu_custom_call" | custom-call | tf_op jit(solution)/shard_map/pallas_call | solution.py:332
  61.9 1.0 %shard_map.104 = (f32[512,256]{1,0:T(8,128)}, f32[256,256]{1,0:T(8,128)}, f32[256,256]{1,0:T(8,128)}) custom-call(f32[512,256]{1,0:T(8,128)S(1)} %get-tuple-element.6.refs_0_, f32[256,256]{1,0:T(8,128)S(1)} %get-tuple-element.7.refs_1_, f32[256,256]{1,0:T(8,128)S(1)} %get-tuple-element.8.refs_2_), custom_call_target="tpu_custom_call" | custom-call | tf_op jit(solution)/shard_map/pallas_call | solution.py:360

commit v4 on v2

--- a/solution.py
+++ b/solution.py
@@ -230,8 +230,12 @@
     loads[2].wait()
     loads[3].wait()
     pre = matmul(spread_in, theta_one[...])
-    grow = jnp.exp(jnp.minimum(pre, 0.0))
-    hidden = jnp.where(pre > 0, pre, grow - 1.0)
+    below = jnp.minimum(pre, 0.0)
+    grow = jnp.exp(below)
+    series = 1.0 + below / 7
+    for k in (6, 5, 4, 3, 2):
+        series = 1.0 + below * series * (1.0 / k)
+    hidden = jnp.where(pre > 0, pre, jnp.where(below > -0.25, below * series, grow - 1.0))
     slope = jnp.where(pre > 0, 1.0, grow)
     hidden_t, spread_in_t = hidden.T, spread_in.T
     pulled = 0.0

time: 63.2 us -> 63.2 us (level)
  no operation moved by 1% of the time
where the time goes in v4:
time: 63.2 us; the launch traced here: 63.1 us
  Pallas kernels  62.3 us (99%)
  between operations  0.8 us (1%)
    pallas_call x1, Pallas kernels, body(): pl.pallas_call(functools.partial(kernel, n, slots), out_shape=(jax.ShapeD...  61.3 us

profile of v4, /device:TPU:1, one launch (start us, length us, event | category | flops | bytes accessed | tf_op | source)
XLA Modules:
  0.0 63.1 jit_solution(11565574341409820227)
XLA Ops:
  0.6 61.3 %shard_map.103 = (f32[512,256]{1,0:T(8,128)S(1)}, f32[256,256]{1,0:T(8,128)S(1)}, f32[256,256]{1,0:T(8,128)S(1)}) custom-call(f32[512,256]{1,0:T(8,128)} %refs_0_.1, s32[4,128]{1,0:T(4,128)} %bitcast.3, f32[256,256]{1,0:T(8,128)} %refs_2_.1, f32[256,256]{1,0:T(8,128)} %refs_3_.1, f32[512,256]{1,0:T(8,128)} %refs_4_.1, s32[1,4,128]{2,1,0:T(4,128)} %bitcast.4, ...), custom_call_target="tpu_custom_call" | custom-call | tf_op jit(solution)/shard_map/pallas_call | solution.py:326
  61.9 1.0 %shard_map.104 = (f32[512,256]{1,0:T(8,128)}, f32[256,256]{1,0:T(8,128)}, f32[256,256]{1,0:T(8,128)}) custom-call(f32[512,256]{1,0:T(8,128)S(1)} %get-tuple-element.6.refs_0_, f32[256,256]{1,0:T(8,128)S(1)} %get-tuple-element.7.refs_1_, f32[256,256]{1,0:T(8,128)S(1)} %get-tuple-element.8.refs_2_), custom_call_target="tpu_custom_call" | custom-call | tf_op jit(solution)/shard_map/pallas_call | solution.py:354

commit v5 on v4

--- a/solution.py
+++ b/solution.py
@@ -170,11 +170,17 @@
     keep_rows = keep[...].astype(F32)
     keep_f = jnp.concatenate([as_column(keep_rows[r : r + 1]) for r in range(nodes // n)], axis=0)
 
-    def load_out(u, field):
-        rows = pick(gather[...], columns(field, u) * node_scale)
+    def channels(ref, u):
+        return ref[UNITS[u][0] * lanes : (UNITS[u][-1] + 1) * lanes, :]
+
+    def load_part(u, part):
+        rows = pick(gather[...], part * node_scale)
         for j in range(slots):
             part = rows[j * n : (j + 1) * n]
             put(down[u], j, jnp.where(live[j], part, jnp.inf) if u == 0 else part)
+
+    def load_out(u, field):
+        load_part(u, columns(field, u))
 
     def send_down(u):
         exchange(2 * u + 4, down[u], there[u])
@@ -238,15 +244,23 @@
     hidden = jnp.where(pre > 0, pre, jnp.where(below > -0.25, below * series, grow - 1.0))
     slope = jnp.where(pre > 0, 1.0, grow)
     hidden_t, spread_in_t = hidden.T, spread_in.T
-    pulled = 0.0
+    pulled = [0.0] * len(units_c)
     for u in units_b:
         spread_cot = propagated(u)
-        pulled += matmul(spread_cot, columns(theta_two[...], u), ((1,), (1,)))
         if u != units_b[-1]:
+            for k, c in enumerate(units_c):
+                pulled[k] += matmul(spread_cot, columns(channels(theta_two, c), u), ((1,), (1,)))
             set_term(1, UNITS[u], matmul(hidden_t, spread_cot))
-    grad_pre = pulled * slope
-    load_out(units_c[0], grad_pre)
+
+    def grad_part(c):
+        pull = matmul(spread_cot, columns(channels(theta_two, c), units_b[-1]), ((1,), (1,)))
+        return (pulled[c - first_c] + pull) * columns(slope, c)
+
+    grad_parts = [grad_part(units_c[0])]
+    load_part(units_c[0], grad_parts[0])
     send_down(units_c[0])
+    grad_parts += [grad_part(c) for c in units_c[1:]]
+    grad_pre = jnp.concatenate(grad_parts, axis=1)
 
     set_term(1, UNITS[units_b[-1]], matmul(hidden_t, spread_cot))
     set_term(0, (0, 1), matmul(spread_in_t, grad_pre))

time: 63.2 us -> 63.1 us (level)
  no operation moved by 1% of the time
where the time goes in v5:
time: 63.1 us; the launch traced here: 63 us
  Pallas kernels  62.2 us (99%)
  between operations  0.8 us (1%)
    pallas_call x1, Pallas kernels, body(): pl.pallas_call(functools.partial(kernel, n, slots), out_shape=(jax.ShapeD...  61.2 us

profile of v5, /device:TPU:1, one launch (start us, length us, event | category | flops | bytes accessed | tf_op | source)
XLA Modules:
  0.0 63.0 jit_solution(8534768957450765587)
XLA Ops:
  0.6 61.2 %shard_map.103 = (f32[512,256]{1,0:T(8,128)S(1)}, f32[256,256]{1,0:T(8,128)S(1)}, f32[256,256]{1,0:T(8,128)S(1)}) custom-call(f32[512,256]{1,0:T(8,128)} %refs_0_.1, s32[4,128]{1,0:T(4,128)} %bitcast.3, f32[256,256]{1,0:T(8,128)} %refs_2_.1, f32[256,256]{1,0:T(8,128)} %refs_3_.1, f32[512,256]{1,0:T(8,128)} %refs_4_.1, s32[1,4,128]{2,1,0:T(4,128)} %bitcast.4, ...), custom_call_target="tpu_custom_call" | custom-call | tf_op jit(solution)/shard_map/pallas_call | solution.py:340
  61.8 1.0 %shard_map.104 = (f32[512,256]{1,0:T(8,128)}, f32[256,256]{1,0:T(8,128)}, f32[256,256]{1,0:T(8,128)}) custom-call(f32[512,256]{1,0:T(8,128)S(1)} %get-tuple-element.6.refs_0_, f32[256,256]{1,0:T(8,128)S(1)} %get-tuple-element.7.refs_1_, f32[256,256]{1,0:T(8,128)S(1)} %get-tuple-element.8.refs_2_), custom_call_target="tpu_custom_call" | custom-call | tf_op jit(solution)/shard_map/pallas_call | solution.py:368
